TPU v7x, 32 devices: a whole 2x2x4 slice. The times are simulated.
32 devices in a mesh: chan: 16 (over z, x, core), tm: 2 (over y).
Axes of the slice: x: 2, y: 2, z: 4, core: 2. Of those that a mesh axis runs over, the one named last changes fastest.
Arguments:
- raw_strain: bfloat16 [2048, 16384], P('chan', 'tm'), may hold values from -6 to 6
- fir_taps: bfloat16 [64], replicated, may hold values from -0.75 to 0.75
- sources: int32 [2, 8], replicated, may hold values from 0 to 2047, as said below
Outputs:
- correlation: float32 [2, 8, 257, 2048], P(None, 'tm', None, 'chan')
Inputs may be any that keep to these rules, and one draw needn't show every extreme that they name: `sources`: the 16 entries are distinct channel indices; the first and the last channel are always among them.
All inputs are finite; a program needn't handle non-finite values.
Results may differ from a plain program's by a relative error of at most 0.0037.
Values may be sent and summed in bfloat16 or wider, within the bound.
A program may use at most 64 MiB of HBM per device.

v0:
```python
import math
import jax
import jax.numpy as jnp
from jax import lax
from jax.sharding import PartitionSpec as P

TAPS = 64
DECIM = 4
HALF_WIN = 32
LAGS = 257
HALF_LAG = 128
STEPS = 2
tile_width = 128


def shifted(x, axis, by):
    length = lax.axis_size(axis)
    pairs = [(i, i + by) for i in range(length) if 0 <= i + by < length]
    return lax.ppermute(x, axis, pairs)


def padded_2(x, sides, width):
    for axis, dim in sides:
        size, length = (lax.axis_size(axis), x.shape[dim])
        up = [(i, (i + 1) % size) for i in range(size - 1)]
        down = [(j, i) for i, j in up]
        last = lax.slice_in_dim(x, length - width, length, axis=dim)
        initial = lax.slice_in_dim(x, 0, width, axis=dim)
        before = lax.ppermute(last, axis, up)
        after = lax.ppermute(initial, axis, down)
        x = jnp.concatenate([before, x, after], axis=dim)
    return x


def filter_matrix(fir_taps, phases, guard_width):
    count = fir_taps.shape[0]
    offset = jnp.arange(tile_width + guard_width)[:, None, None]
    phase_ids = jnp.arange(phases)[None, :, None]
    column = jnp.arange(tile_width)[None, None, :]
    tap_index = count - phases * (offset - column) - phase_ids
    matches = tap_index[..., None] == jnp.arange(count)[None, None, None, :]
    weights = jnp.sum(jnp.where(matches, fir_taps.astype(jnp.float32), 0.0), axis=-1)
    return weights.astype(jnp.bfloat16).reshape((tile_width + guard_width) * phases, tile_width)


def decimate(extended, fir_taps, outputs):
    phases = DECIM
    guard_width = TAPS // DECIM
    channel_count = extended.shape[0]
    block_count = outputs // tile_width
    polyphase = extended.reshape(channel_count, outputs + guard_width, phases)
    padded = jnp.pad(polyphase, ((0, 0), (0, tile_width - guard_width), (0, 0)))
    leading = padded[:, :outputs].reshape(channel_count, block_count, tile_width, phases)
    trailing = padded[:, tile_width : tile_width + outputs].reshape(
        channel_count, block_count, tile_width, phases
    )
    blocks = jnp.concatenate([leading, trailing[:, :, :guard_width]], axis=2)
    blocks = blocks.reshape(channel_count, block_count, (tile_width + guard_width) * phases)
    result = jnp.einsum(
        "cbj,ji->cbi",
        blocks,
        filter_matrix(fir_taps, phases, guard_width),
        preferred_element_type=jnp.float32,
    )
    return result.reshape(channel_count, outputs)


def window_sums(magnitude, outputs):
    span_width = 2 * HALF_WIN
    channel_count = magnitude.shape[0]
    block_count = outputs // tile_width
    padded = jnp.pad(magnitude, ((0, 0), (0, tile_width - span_width)))
    leading = padded[:, :outputs].reshape(channel_count, block_count, tile_width)
    trailing = padded[:, tile_width : tile_width + outputs].reshape(
        channel_count, block_count, tile_width
    )
    blocks = jnp.concatenate([leading, trailing[:, :, :span_width]], axis=2)
    row_ids = jnp.arange(tile_width + span_width)[:, None]
    col_ids = jnp.arange(tile_width)[None, :]
    band = ((row_ids >= col_ids) & (row_ids <= col_ids + span_width)).astype(jnp.float32)
    sums = jnp.einsum(
        "cbj,ji->cbi",
        blocks,
        band,
        precision=lax.Precision.HIGHEST,
        preferred_element_type=jnp.float32,
    )
    return sums.reshape(channel_count, outputs)


def lag_products(extended_traces, receivers):
    length = receivers.shape[1]
    width = length + LAGS - 1

    def single(trace):
        tiled = jnp.tile(trace, LAGS + 1)[: LAGS * (width + 1)].reshape(LAGS, width + 1)
        toeplitz = tiled[::-1, :length]
        return jnp.einsum("lm,rm->lr", toeplitz, receivers, preferred_element_type=jnp.float32)

    return lax.map(single, extended_traces)


def per_device(raw_strain, fir_taps, sources):
    dec_dev = raw_strain.shape[1] // DECIM
    left_rim = shifted(raw_strain[:, raw_strain.shape[1] - TAPS :], "tm", 1)
    decimated = decimate(jnp.concatenate([left_rim, raw_strain], axis=1), fir_taps, dec_dev)
    beside_all = padded_2(decimated, (("tm", 1),), HALF_WIN)
    magnitude = jnp.abs(beside_all)
    level = window_sums(magnitude, dec_dev) / (2 * HALF_WIN + 1) + 1e-05
    white = (decimated / level).astype(jnp.bfloat16)
    channel_count = white.shape[0]
    my_block = lax.axis_index("chan")
    owner_ids = sources // channel_count
    local_rows = sources % channel_count
    traces = []
    for step_index in range(STEPS):
        picks = (local_rows[step_index][:, None] == jnp.arange(channel_count)[None, :]) & (
            owner_ids[step_index][:, None] == my_block
        )
        summed = lax.psum(
            jnp.dot(picks.astype(jnp.bfloat16), white, preferred_element_type=jnp.float32), "chan"
        )
        traces.append(summed.astype(jnp.bfloat16))
    scale = 1.0 / math.sqrt(dec_dev * lax.axis_size("tm"))
    terms = []
    for step_index in range(STEPS):
        extended = padded_2(traces[step_index], (("tm", 1),), HALF_LAG)
        terms.append(lag_products(extended, white) * scale)
    return lax.psum_scatter(jnp.stack(terms), "tm", scatter_dimension=1, tiled=True)


def solution(mesh):
    placed = (P("chan", "tm"), P(), P())
    return jax.shard_map(
        per_device,
        mesh=mesh,
        in_specs=placed,
        out_specs=P(None, "tm", None, "chan"),
        check_vma=False,
    )
```

profile of v0, /device:TPU:0, one launch (start us, length us, event | category | flops | bytes accessed | tf_op | source)
XLA Modules:
  0.0 399.5 jit_solution(1200064050294466446)
XLA Ops:
  9.8 4.9 %collective-permute-start = (bf16[128,64]{0,1:T(8,128)(2,1)S(1)}, bf16[128,64]{0,1:T(8,128)(2,1)S(1)}, u32[]{:S(2)}, u32[]{:S(2)}) collective-permute-start(bf16[128,64]{0,1:T(8,128)(2,1)S(1)} %slice.86), channel_id=1, source_target_pairs={{0,1},{2,3},{4,5},{6,7},{8,9},{10,11},{12,13},{14,15},{16,17},{18,... | collective-permute-start | bytes 49160 | tf_op jit(solution)/shard_map/ppermute | solution.py:19
  14.8 6.9 %select_reduce_fusion = bf16[144,4,128]{2,1,0:T(4,128)(2,1)S(1)} fusion(f32[64]{0:T(128)S(1)} %convert_element_type.22, s32[144,4,128]{2,1,0:T(4,128)S(1)} %iota_subtract_fusion), kind=kLoop, calls=%fused_computation.4 | loop fusion | flops 14082048 | bytes 442624 | tf_op jit(solution)/shard_map/reduce_sum | solution.py:42
  36.9 60.9 %all-reduce.8 = (bf16[8,2048]{1,0:T(8,128)(2,1)S(1)}, bf16[8,2048]{1,0:T(8,128)(2,1)S(1)}) all-reduce(f32[8,2048]{1,0:T(8,128)S(1)} %fusion.24, f32[8,2048]{1,0:T(8,128)S(1)} %fusion.21), channel_id=1, replica_groups=mesh['chan'=16,'tm'=2] {'chan'}, use_global_device_ids=true, to_apply=%region_4.5 | all-reduce | flops 32768 | bytes 196608 | tf_op jit(solution)/shard_map/psum | solution.py:120
  101.0 4.5 %collective-permute-start.5 = (bf16[8,128]{1,0:T(8,128)(2,1)S(1)}, bf16[8,128]{1,0:T(8,128)(2,1)S(1)}, u32[]{:S(2)}, u32[]{:S(2)}) collective-permute-start(bf16[8,128]{1,0:T(8,128)(2,1)S(1)} %get-tuple-element.77), channel_id=1, source_target_pairs={{0,1},{2,3},{4,5},{6,7},{8,9},{10,11},{12,13},{14,15},{16,17},{18,... | collective-permute-start | bytes 6152 | tf_op jit(solution)/shard_map/ppermute | solution.py:29
  108.1 107.8 %while.20 = (s32[]{:T(128)}, f32[8,257,128]{2,0,1:T(8,128)}, bf16[8,2304]{1,0:T(8,128)(2,1)S(1)}, bf16[128,2048]{1,0:T(8,128)(2,1)S(1)}, s32[]{:T(128)}, /*index=5*/s32[]{:T(128)}) while((s32[]{:T(128)}, f32[8,257,128]{2,0,1:T(8,128)}, bf16[8,2304]{1,0:T(8,128)(2,1)S(1)}, bf16[128,2048]{1,0:T(8,128)(2,1)S(1)}, s32[]{:T(128)}, ...), condition=%wide.region_3.4_spmd, body=%wide.region_2.3_spmd.sunk | while | flops 134742016 | bytes 14765141 | solution.py:100
  112.0 4.0 rev.8
  116.6 5.0 %dynamic_update_slice.9 = f32[8,257,128]{2,0,1:T(8,128)} dynamic-update-slice(f32[8,257,128]{2,0,1:T(8,128)} %get-tuple-element.162, f32[1,257,128]{2,0,1:T(1,128)S(1)} %copy.59, s32[]{:T(128)} %get-tuple-element.161, s32[]{:T(128)} %constant.54.clone.1..sunk, s32[]{:T(128)} %constant.54.clone.1..sunk) | dynamic-update-slice | bytes 263172 | tf_op jit(solution)/shard_map/while/body/jit(dynamic_update_index_in_dim)/dynamic_update_slice | solution.py:100
  130.1 5.0 %dynamic_update_slice.9 = f32[8,257,128]{2,0,1:T(8,128)} dynamic-update-slice(f32[8,257,128]{2,0,1:T(8,128)} %get-tuple-element.162, f32[1,257,128]{2,0,1:T(1,128)S(1)} %copy.59, s32[]{:T(128)} %get-tuple-element.161, s32[]{:T(128)} %constant.54.clone.1..sunk, s32[]{:T(128)} %constant.54.clone.1..sunk) | dynamic-update-slice | bytes 263172 | tf_op jit(solution)/shard_map/while/body/jit(dynamic_update_index_in_dim)/dynamic_update_slice | solution.py:100
  138.9 4.0 rev.8
  143.5 5.0 %dynamic_update_slice.9 = f32[8,257,128]{2,0,1:T(8,128)} dynamic-update-slice(f32[8,257,128]{2,0,1:T(8,128)} %get-tuple-element.162, f32[1,257,128]{2,0,1:T(1,128)S(1)} %copy.59, s32[]{:T(128)} %get-tuple-element.161, s32[]{:T(128)} %constant.54.clone.1..sunk, s32[]{:T(128)} %constant.54.clone.1..sunk) | dynamic-update-slice | bytes 263172 | tf_op jit(solution)/shard_map/while/body/jit(dynamic_update_index_in_dim)/dynamic_update_slice | solution.py:100
  152.4 4.0 rev.8
  157.0 5.0 %dynamic_update_slice.9 = f32[8,257,128]{2,0,1:T(8,128)} dynamic-update-slice(f32[8,257,128]{2,0,1:T(8,128)} %get-tuple-element.162, f32[1,257,128]{2,0,1:T(1,128)S(1)} %copy.59, s32[]{:T(128)} %get-tuple-element.161, s32[]{:T(128)} %constant.54.clone.1..sunk, s32[]{:T(128)} %constant.54.clone.1..sunk) | dynamic-update-slice | bytes 263172 | tf_op jit(solution)/shard_map/while/body/jit(dynamic_update_index_in_dim)/dynamic_update_slice | solution.py:100
  165.9 4.0 rev.8
  170.5 5.0 %dynamic_update_slice.9 = f32[8,257,128]{2,0,1:T(8,128)} dynamic-update-slice(f32[8,257,128]{2,0,1:T(8,128)} %get-tuple-element.162, f32[1,257,128]{2,0,1:T(1,128)S(1)} %copy.59, s32[]{:T(128)} %get-tuple-element.161, s32[]{:T(128)} %constant.54.clone.1..sunk, s32[]{:T(128)} %constant.54.clone.1..sunk) | dynamic-update-slice | bytes 263172 | tf_op jit(solution)/shard_map/while/body/jit(dynamic_update_index_in_dim)/dynamic_update_slice | solution.py:100
  179.3 4.0 rev.8
  184.0 5.0 %dynamic_update_slice.9 = f32[8,257,128]{2,0,1:T(8,128)} dynamic-update-slice(f32[8,257,128]{2,0,1:T(8,128)} %get-tuple-element.162, f32[1,257,128]{2,0,1:T(1,128)S(1)} %copy.59, s32[]{:T(128)} %get-tuple-element.161, s32[]{:T(128)} %constant.54.clone.1..sunk, s32[]{:T(128)} %constant.54.clone.1..sunk) | dynamic-update-slice | bytes 263172 | tf_op jit(solution)/shard_map/while/body/jit(dynamic_update_index_in_dim)/dynamic_update_slice | solution.py:100
  192.8 4.0 rev.8
  197.4 5.0 %dynamic_update_slice.9 = f32[8,257,128]{2,0,1:T(8,128)} dynamic-update-slice(f32[8,257,128]{2,0,1:T(8,128)} %get-tuple-element.162, f32[1,257,128]{2,0,1:T(1,128)S(1)} %copy.59, s32[]{:T(128)} %get-tuple-element.161, s32[]{:T(128)} %constant.54.clone.1..sunk, s32[]{:T(128)} %constant.54.clone.1..sunk) | dynamic-update-slice | bytes 263172 | tf_op jit(solution)/shard_map/while/body/jit(dynamic_update_index_in_dim)/dynamic_update_slice | solution.py:100
  206.3 4.0 rev.8
  210.9 5.0 %dynamic_update_slice.9 = f32[8,257,128]{2,0,1:T(8,128)} dynamic-update-slice(f32[8,257,128]{2,0,1:T(8,128)} %get-tuple-element.162, f32[1,257,128]{2,0,1:T(1,128)S(1)} %copy.59, s32[]{:T(128)} %get-tuple-element.161, s32[]{:T(128)} %constant.54.clone.1..sunk, s32[]{:T(128)} %constant.54.clone.1..sunk) | dynamic-update-slice | bytes 263172 | tf_op jit(solution)/shard_map/while/body/jit(dynamic_update_index_in_dim)/dynamic_update_slice | solution.py:100
  217.0 108.1 %while.21 = (s32[]{:T(128)}, f32[8,257,128]{2,0,1:T(8,128)}, bf16[8,2304]{1,0:T(8,128)(2,1)S(1)}, bf16[128,2048]{1,0:T(8,128)(2,1)S(1)}, s32[]{:T(128)}, /*index=5*/s32[]{:T(128)}) while((s32[]{:T(128)}, f32[8,257,128]{2,0,1:T(8,128)}, bf16[8,2304]{1,0:T(8,128)(2,1)S(1)}, bf16[128,2048]{1,0:T(8,128)(2,1)S(1)}, s32[]{:T(128)}, ...), condition=%wide.region_6.7_spmd, body=%wide.region_5.6_spmd.sunk | while | flops 134742016 | bytes 14765141 | solution.py:100
  220.8 4.0 rev.9
  225.4 5.0 %dynamic_update_slice.10 = f32[8,257,128]{2,0,1:T(8,128)} dynamic-update-slice(f32[8,257,128]{2,0,1:T(8,128)} %get-tuple-element.144, f32[1,257,128]{2,0,1:T(1,128)S(1)} %copy.60, s32[]{:T(128)} %get-tuple-element.143, s32[]{:T(128)} %constant.54.clone.1..sunk.1, s32[]{:T(128)} %constant.54.clone.1..sunk.1) | dynamic-update-slice | bytes 263172 | tf_op jit(solution)/shard_map/while/body/jit(dynamic_update_index_in_dim)/dynamic_update_slice | solution.py:100
  234.3 4.0 rev.9
  238.9 5.0 %dynamic_update_slice.10 = f32[8,257,128]{2,0,1:T(8,128)} dynamic-update-slice(f32[8,257,128]{2,0,1:T(8,128)} %get-tuple-element.144, f32[1,257,128]{2,0,1:T(1,128)S(1)} %copy.60, s32[]{:T(128)} %get-tuple-element.143, s32[]{:T(128)} %constant.54.clone.1..sunk.1, s32[]{:T(128)} %constant.54.clone.1..sunk.1) | dynamic-update-slice | bytes 263172 | tf_op jit(solution)/shard_map/while/body/jit(dynamic_update_index_in_dim)/dynamic_update_slice | solution.py:100
  252.5 5.0 %dynamic_update_slice.10 = f32[8,257,128]{2,0,1:T(8,128)} dynamic-update-slice(f32[8,257,128]{2,0,1:T(8,128)} %get-tuple-element.144, f32[1,257,128]{2,0,1:T(1,128)S(1)} %copy.60, s32[]{:T(128)} %get-tuple-element.143, s32[]{:T(128)} %constant.54.clone.1..sunk.1, s32[]{:T(128)} %constant.54.clone.1..sunk.1) | dynamic-update-slice | bytes 263172 | tf_op jit(solution)/shard_map/while/body/jit(dynamic_update_index_in_dim)/dynamic_update_slice | solution.py:100
  266.0 5.0 %dynamic_update_slice.10 = f32[8,257,128]{2,0,1:T(8,128)} dynamic-update-slice(f32[8,257,128]{2,0,1:T(8,128)} %get-tuple-element.144, f32[1,257,128]{2,0,1:T(1,128)S(1)} %copy.60, s32[]{:T(128)} %get-tuple-element.143, s32[]{:T(128)} %constant.54.clone.1..sunk.1, s32[]{:T(128)} %constant.54.clone.1..sunk.1) | dynamic-update-slice | bytes 263172 | tf_op jit(solution)/shard_map/while/body/jit(dynamic_update_index_in_dim)/dynamic_update_slice | solution.py:100
  279.5 5.0 %dynamic_update_slice.10 = f32[8,257,128]{2,0,1:T(8,128)} dynamic-update-slice(f32[8,257,128]{2,0,1:T(8,128)} %get-tuple-element.144, f32[1,257,128]{2,0,1:T(1,128)S(1)} %copy.60, s32[]{:T(128)} %get-tuple-element.143, s32[]{:T(128)} %constant.54.clone.1..sunk.1, s32[]{:T(128)} %constant.54.clone.1..sunk.1) | dynamic-update-slice | bytes 263172 | tf_op jit(solution)/shard_map/while/body/jit(dynamic_update_index_in_dim)/dynamic_update_slice | solution.py:100
  293.0 5.0 %dynamic_update_slice.10 = f32[8,257,128]{2,0,1:T(8,128)} dynamic-update-slice(f32[8,257,128]{2,0,1:T(8,128)} %get-tuple-element.144, f32[1,257,128]{2,0,1:T(1,128)S(1)} %copy.60, s32[]{:T(128)} %get-tuple-element.143, s32[]{:T(128)} %constant.54.clone.1..sunk.1, s32[]{:T(128)} %constant.54.clone.1..sunk.1) | dynamic-update-slice | bytes 263172 | tf_op jit(solution)/shard_map/while/body/jit(dynamic_update_index_in_dim)/dynamic_update_slice | solution.py:100
  306.5 5.0 %dynamic_update_slice.10 = f32[8,257,128]{2,0,1:T(8,128)} dynamic-update-slice(f32[8,257,128]{2,0,1:T(8,128)} %get-tuple-element.144, f32[1,257,128]{2,0,1:T(1,128)S(1)} %copy.60, s32[]{:T(128)} %get-tuple-element.143, s32[]{:T(128)} %constant.54.clone.1..sunk.1, s32[]{:T(128)} %constant.54.clone.1..sunk.1) | dynamic-update-slice | bytes 263172 | tf_op jit(solution)/shard_map/while/body/jit(dynamic_update_index_in_dim)/dynamic_update_slice | solution.py:100
  320.0 5.0 %dynamic_update_slice.10 = f32[8,257,128]{2,0,1:T(8,128)} dynamic-update-slice(f32[8,257,128]{2,0,1:T(8,128)} %get-tuple-element.144, f32[1,257,128]{2,0,1:T(1,128)S(1)} %copy.60, s32[]{:T(128)} %get-tuple-element.143, s32[]{:T(128)} %constant.54.clone.1..sunk.1, s32[]{:T(128)} %constant.54.clone.1..sunk.1) | dynamic-update-slice | bytes 263172 | tf_op jit(solution)/shard_map/while/body/jit(dynamic_update_index_in_dim)/dynamic_update_slice | solution.py:100
  330.1 59.8 %all-reduce.7.cloned.1.call-done = f32[2,8,257,128]{3,1,2,0:T(8,128)} async-done(((f32[2,8,257,128]{3,1,2,0:T(8,128)}), f32[2,8,257,128]{3,1,2,0:T(8,128)}) %all-reduce.7.cloned.1.call-update) | async-done | bytes 2105360
  (190 shorter events, 131.0 us)
Async XLA Ops:
  6.5 8.2 %copy-start.1 = (bf16[64]{0:T(256)(128)(2,1)S(1)}, bf16[64]{0:T(256)(128)(2,1)}, u32[]{:S(2)}) copy-start(bf16[64]{0:T(256)(128)(2,1)} %param.8) | copy-start | bytes 388
  6.5 8.3 %copy-start = (s32[2,8]{1,0:T(2,128)S(1)}, s32[2,8]{1,0:T(2,128)}, u32[]{:S(2)}) copy-start(s32[2,8]{1,0:T(2,128)} %param.9) | copy-start | bytes 196
  6.5 383.4 %all-reduce.7.cloned.1.call-start = ((), (), s32[]{:S(2)}) async-start(), calls=%async_computation | async-start | bytes 4210688
  9.8 12.0 %collective-permute-start = (bf16[128,64]{0,1:T(8,128)(2,1)S(1)}, bf16[128,64]{0,1:T(8,128)(2,1)S(1)}, u32[]{:S(2)}, u32[]{:S(2)}) collective-permute-start(bf16[128,64]{0,1:T(8,128)(2,1)S(1)} %slice.86), channel_id=1, source_target_pairs={{0,1},{2,3},{4,5},{6,7},{8,9},{10,11},{12,13},{14,15},{16,17},{18,... | collective-permute-start | bytes 49160 | tf_op jit(solution)/shard_map/ppermute | solution.py:19
  25.6 3.0 collective-permute-start.1
  26.9 5.6 %collective-permute-start.2 = (f32[128,32]{0,1:T(8,128)S(1)}, f32[128,32]{0,1:T(8,128)S(1)}, u32[]{:S(2)}, u32[]{:S(2)}) collective-permute-start(f32[128,32]{0,1:T(8,128)S(1)} %get-tuple-element.74), channel_id=1, source_target_pairs={{1,0},{3,2},{5,4},{7,6},{9,8},{11,10},{13,12},{15,14},{17,16},{19,... | collective-permute-start | bytes 49160 | tf_op jit(solution)/shard_map/ppermute | solution.py:30
  97.8 9.3 %collective-permute-start.3 = (bf16[8,128]{1,0:T(8,128)(2,1)S(1)}, bf16[8,128]{1,0:T(8,128)(2,1)S(1)}, u32[]{:S(2)}, u32[]{:S(2)}) collective-permute-start(bf16[8,128]{1,0:T(8,128)(2,1)S(1)} %get-tuple-element.75), channel_id=1, source_target_pairs={{0,1},{2,3},{4,5},{6,7},{8,9},{10,11},{12,13},{14,15},{16,17},{18,... | collective-permute-start | bytes 6152 | tf_op jit(solution)/shard_map/ppermute | solution.py:29
  99.7 7.4 %collective-permute-start.4 = (bf16[8,128]{1,0:T(8,128)(2,1)S(1)}, bf16[8,128]{1,0:T(8,128)(2,1)S(1)}, u32[]{:S(2)}, u32[]{:S(2)}) collective-permute-start(bf16[8,128]{1,0:T(8,128)(2,1)S(1)} %get-tuple-element.76), channel_id=1, source_target_pairs={{1,0},{3,2},{5,4},{7,6},{9,8},{11,10},{13,12},{15,14},{17,16},{19,... | collective-permute-start | bytes 6152 | tf_op jit(solution)/shard_map/ppermute | solution.py:30
  101.0 114.9 %collective-permute-start.5 = (bf16[8,128]{1,0:T(8,128)(2,1)S(1)}, bf16[8,128]{1,0:T(8,128)(2,1)S(1)}, u32[]{:S(2)}, u32[]{:S(2)}) collective-permute-start(bf16[8,128]{1,0:T(8,128)(2,1)S(1)} %get-tuple-element.77), channel_id=1, source_target_pairs={{0,1},{2,3},{4,5},{6,7},{8,9},{10,11},{12,13},{14,15},{16,17},{18,... | collective-permute-start | bytes 6152 | tf_op jit(solution)/shard_map/ppermute | solution.py:29
  105.6 110.4 %collective-permute-start.6 = (bf16[8,128]{1,0:T(8,128)(2,1)S(1)}, bf16[8,128]{1,0:T(8,128)(2,1)S(1)}, u32[]{:S(2)}, u32[]{:S(2)}) collective-permute-start(bf16[8,128]{1,0:T(8,128)(2,1)S(1)} %get-tuple-element.78), channel_id=1, source_target_pairs={{1,0},{3,2},{5,4},{7,6},{9,8},{11,10},{13,12},{15,14},{17,16},{19,... | collective-permute-start | bytes 6152 | tf_op jit(solution)/shard_map/ppermute | solution.py:30
  328.2 0.7 copy-start.2
Sparse Core Ops, SparseCore 0:
  328.4 61.4 all-reduce.6
where the time goes:
time: 402 us; the launch traced here: 399 us
  local copies, waits for them, and re-layouts  221 us (55%)
  waiting for transfers between devices  63.8 us (16%)
  blocking collectives  60.9 us (15%)
  starting transfers between devices  16.7 us (4%)
  between operations  14.4 us (4%)
  other arithmetic  11.8 us (3%)
  matrix products  9.57 us (2%)
    dynamic_update_slice x32, local copies, waits for them, and re-layouts, lag_products(): return lax.map(single, extended_traces)  82.6 us
    rev x16, local copies, waits for them, and re-layouts, single(): toeplitz = tiled[::-1, :length]  63.6 us
    psum x1, blocking collectives, per_device(): lax.psum(jnp.dot(picks.astype(jnp.bfloat16), white, preferred_element_typ...  60.9 us
    unnamed x2, waiting for transfers between devices  59.8 us
    reshape x16, local copies, waits for them, and re-layouts, single(): jnp.tile(trace, LAGS + 1)[:LAGS * (width + 1)].reshape(LAGS, width + 1)  33.7 us
    another operation x32, local copies, waits for them, and re-layouts, single(): jnp.tile(trace, LAGS + 1)[:LAGS * (width + 1)].reshape(LAGS, width + 1)  23.4 us
  transfers between devices with their start and end apart: 8, of which 2 were waited for; matrix products, arithmetic and copies ran while one was open for 29% of the time, Pallas kernels for 0%

commit v1 on v0

--- a/solution.py
+++ b/solution.py
@@ -117,8 +117,12 @@
         picks = (local_rows[step_index][:, None] == jnp.arange(channel_count)[None, :]) & (
             owner_ids[step_index][:, None] == my_block
         )
-        summed = lax.psum(
-            jnp.dot(picks.astype(jnp.bfloat16), white, preferred_element_type=jnp.float32), "chan"
+        summed = jnp.sum(
+            lax.all_gather(
+                jnp.dot(picks.astype(jnp.bfloat16), white, preferred_element_type=jnp.float32),
+                "chan",
+            ),
+            axis=0,
         )
         traces.append(summed.astype(jnp.bfloat16))
     scale = 1.0 / math.sqrt(dec_dev * lax.axis_size("tm"))

time: 402 us -> 417 us (1.037)
  waiting for transfers between devices: 63.8 us -> 136 us
  blocking collectives: 60.9 us -> 0 us
    all_gather x0 -> x2, waiting for transfers between devices: none -> 70.5 us  [per_device(): lax.all_gather(jnp.dot(picks.astype(jnp.bfloat16), white, preferred_eleme...]
    psum x1 -> x0, blocking collectives: 60.9 us -> none  [per_device(): lax.psum(jnp.dot(picks.astype(jnp.bfloat16), white, preferred_element_typ...]
    unnamed x2 -> x4, waiting for transfers between devices: 59.8 us -> 61.5 us
  transfers between devices with their start and end apart: 8 -> 10, of which waited for: 2 -> 4; matrix products, arithmetic and copies ran while one was open for 29% -> 29% of each run, Pallas kernels for 0% -> 0%
where the time goes in v1:
time: 417 us; the launch traced here: 415 us
  local copies, waits for them, and re-layouts  221 us (53%)
  waiting for transfers between devices  136 us (33%)
  starting transfers between devices  17.1 us (4%)
  other arithmetic  14.4 us (3%)
  between operations  14.1 us (3%)
  matrix products  10.8 us (3%)
    dynamic_update_slice x32, local copies, waits for them, and re-layouts, lag_products(): return lax.map(single, extended_traces)  82.6 us
    all_gather x2, waiting for transfers between devices, per_device(): lax.all_gather(jnp.dot(picks.astype(jnp.bfloat16), white, preferred_eleme...  70.5 us
    rev x16, local copies, waits for them, and re-layouts, single(): toeplitz = tiled[::-1, :length]  63.6 us
    unnamed x4, waiting for transfers between devices  61.5 us
    reshape x16, local copies, waits for them, and re-layouts, single(): jnp.tile(trace, LAGS + 1)[:LAGS * (width + 1)].reshape(LAGS, width + 1)  33.7 us
    another operation x32, local copies, waits for them, and re-layouts, single(): jnp.tile(trace, LAGS + 1)[:LAGS * (width + 1)].reshape(LAGS, width + 1)  23.4 us
  transfers between devices with their start and end apart: 10, of which 4 were waited for; matrix products, arithmetic and copies ran while one was open for 29% of the time, Pallas kernels for 0%

profile of v1, /device:TPU:0, one launch (start us, length us, event | category | flops | bytes accessed | tf_op | source)
XLA Modules:
  0.0 414.6 jit_solution(8137210842604876744)
XLA Ops:
  9.8 4.9 %collective-permute-start = (bf16[128,64]{0,1:T(8,128)(2,1)S(1)}, bf16[128,64]{0,1:T(8,128)(2,1)S(1)}, u32[]{:S(2)}, u32[]{:S(2)}) collective-permute-start(bf16[128,64]{0,1:T(8,128)(2,1)S(1)} %slice.86), channel_id=1, source_target_pairs={{0,1},{2,3},{4,5},{6,7},{8,9},{10,11},{12,13},{14,15},{16,17},{18,... | collective-permute-start | bytes 49160 | tf_op jit(solution)/shard_map/ppermute | solution.py:19
  14.8 6.9 %select_reduce_fusion = bf16[144,4,128]{2,1,0:T(4,128)(2,1)S(1)} fusion(f32[64]{0:T(128)S(1)} %convert_element_type.22, s32[144,4,128]{2,1,0:T(4,128)S(1)} %iota_subtract_fusion), kind=kLoop, calls=%fused_computation.4 | loop fusion | flops 14082048 | bytes 442624 | tf_op jit(solution)/shard_map/reduce_sum | solution.py:42
  38.3 37.4 %all-gather.5.cloned.1.call-done = f32[128,2048]{1,0:T(8,128)} async-done(((f32[8,2048]{1,0:T(8,128)}), f32[128,2048]{1,0:T(8,128)}) %all-gather.5.cloned.1.call-update) | async-done | bytes 1048592 | tf_op jit(solution)/shard_map/all_gather | solution.py:121
  81.6 33.1 %all-gather.7.cloned.1.call-done = f32[128,2048]{1,0:T(8,128)} async-done(((f32[8,2048]{1,0:T(8,128)}), f32[128,2048]{1,0:T(8,128)}) %all-gather.7.cloned.1.call-update) | async-done | bytes 1048592 | tf_op jit(solution)/shard_map/all_gather | solution.py:121
  122.0 107.7 %while.20 = (s32[]{:T(128)}, f32[8,257,128]{2,0,1:T(8,128)}, bf16[8,2304]{1,0:T(8,128)(2,1)S(1)}, bf16[128,2048]{1,0:T(8,128)(2,1)S(1)}, s32[]{:T(128)}, /*index=5*/s32[]{:T(128)}) while((s32[]{:T(128)}, f32[8,257,128]{2,0,1:T(8,128)}, bf16[8,2304]{1,0:T(8,128)(2,1)S(1)}, bf16[128,2048]{1,0:T(8,128)(2,1)S(1)}, s32[]{:T(128)}, ...), condition=%wide.region_3.4_spmd, body=%wide.region_2.3_spmd.sunk | while | flops 134742016 | bytes 14765141 | solution.py:100
  125.8 4.0 rev.8
  130.4 5.0 %dynamic_update_slice.9 = f32[8,257,128]{2,0,1:T(8,128)} dynamic-update-slice(f32[8,257,128]{2,0,1:T(8,128)} %get-tuple-element.160, f32[1,257,128]{2,0,1:T(1,128)S(1)} %copy.61, s32[]{:T(128)} %get-tuple-element.159, s32[]{:T(128)} %constant.54.clone.1..sunk, s32[]{:T(128)} %constant.54.clone.1..sunk) | dynamic-update-slice | bytes 263172 | tf_op jit(solution)/shard_map/while/body/jit(dynamic_update_index_in_dim)/dynamic_update_slice | solution.py:100
  139.3 4.0 rev.8
  143.9 5.0 %dynamic_update_slice.9 = f32[8,257,128]{2,0,1:T(8,128)} dynamic-update-slice(f32[8,257,128]{2,0,1:T(8,128)} %get-tuple-element.160, f32[1,257,128]{2,0,1:T(1,128)S(1)} %copy.61, s32[]{:T(128)} %get-tuple-element.159, s32[]{:T(128)} %constant.54.clone.1..sunk, s32[]{:T(128)} %constant.54.clone.1..sunk) | dynamic-update-slice | bytes 263172 | tf_op jit(solution)/shard_map/while/body/jit(dynamic_update_index_in_dim)/dynamic_update_slice | solution.py:100
  152.7 4.0 rev.8
  157.4 5.0 %dynamic_update_slice.9 = f32[8,257,128]{2,0,1:T(8,128)} dynamic-update-slice(f32[8,257,128]{2,0,1:T(8,128)} %get-tuple-element.160, f32[1,257,128]{2,0,1:T(1,128)S(1)} %copy.61, s32[]{:T(128)} %get-tuple-element.159, s32[]{:T(128)} %constant.54.clone.1..sunk, s32[]{:T(128)} %constant.54.clone.1..sunk) | dynamic-update-slice | bytes 263172 | tf_op jit(solution)/shard_map/while/body/jit(dynamic_update_index_in_dim)/dynamic_update_slice | solution.py:100
  166.2 4.0 rev.8
  170.8 5.0 %dynamic_update_slice.9 = f32[8,257,128]{2,0,1:T(8,128)} dynamic-update-slice(f32[8,257,128]{2,0,1:T(8,128)} %get-tuple-element.160, f32[1,257,128]{2,0,1:T(1,128)S(1)} %copy.61, s32[]{:T(128)} %get-tuple-element.159, s32[]{:T(128)} %constant.54.clone.1..sunk, s32[]{:T(128)} %constant.54.clone.1..sunk) | dynamic-update-slice | bytes 263172 | tf_op jit(solution)/shard_map/while/body/jit(dynamic_update_index_in_dim)/dynamic_update_slice | solution.py:100
  184.3 5.0 %dynamic_update_slice.9 = f32[8,257,128]{2,0,1:T(8,128)} dynamic-update-slice(f32[8,257,128]{2,0,1:T(8,128)} %get-tuple-element.160, f32[1,257,128]{2,0,1:T(1,128)S(1)} %copy.61, s32[]{:T(128)} %get-tuple-element.159, s32[]{:T(128)} %constant.54.clone.1..sunk, s32[]{:T(128)} %constant.54.clone.1..sunk) | dynamic-update-slice | bytes 263172 | tf_op jit(solution)/shard_map/while/body/jit(dynamic_update_index_in_dim)/dynamic_update_slice | solution.py:100
  193.1 4.0 rev.8
  197.7 5.0 %dynamic_update_slice.9 = f32[8,257,128]{2,0,1:T(8,128)} dynamic-update-slice(f32[8,257,128]{2,0,1:T(8,128)} %get-tuple-element.160, f32[1,257,128]{2,0,1:T(1,128)S(1)} %copy.61, s32[]{:T(128)} %get-tuple-element.159, s32[]{:T(128)} %constant.54.clone.1..sunk, s32[]{:T(128)} %constant.54.clone.1..sunk) | dynamic-update-slice | bytes 263172 | tf_op jit(solution)/shard_map/while/body/jit(dynamic_update_index_in_dim)/dynamic_update_slice | solution.py:100
  206.6 4.0 rev.8
  211.2 5.0 %dynamic_update_slice.9 = f32[8,257,128]{2,0,1:T(8,128)} dynamic-update-slice(f32[8,257,128]{2,0,1:T(8,128)} %get-tuple-element.160, f32[1,257,128]{2,0,1:T(1,128)S(1)} %copy.61, s32[]{:T(128)} %get-tuple-element.159, s32[]{:T(128)} %constant.54.clone.1..sunk, s32[]{:T(128)} %constant.54.clone.1..sunk) | dynamic-update-slice | bytes 263172 | tf_op jit(solution)/shard_map/while/body/jit(dynamic_update_index_in_dim)/dynamic_update_slice | solution.py:100
  220.1 4.0 rev.8
  224.7 5.0 %dynamic_update_slice.9 = f32[8,257,128]{2,0,1:T(8,128)} dynamic-update-slice(f32[8,257,128]{2,0,1:T(8,128)} %get-tuple-element.160, f32[1,257,128]{2,0,1:T(1,128)S(1)} %copy.61, s32[]{:T(128)} %get-tuple-element.159, s32[]{:T(128)} %constant.54.clone.1..sunk, s32[]{:T(128)} %constant.54.clone.1..sunk) | dynamic-update-slice | bytes 263172 | tf_op jit(solution)/shard_map/while/body/jit(dynamic_update_index_in_dim)/dynamic_update_slice | solution.py:100
  230.7 108.1 %while.21 = (s32[]{:T(128)}, f32[8,257,128]{2,0,1:T(8,128)}, bf16[8,2304]{1,0:T(8,128)(2,1)S(1)}, bf16[128,2048]{1,0:T(8,128)(2,1)S(1)}, s32[]{:T(128)}, /*index=5*/s32[]{:T(128)}) while((s32[]{:T(128)}, f32[8,257,128]{2,0,1:T(8,128)}, bf16[8,2304]{1,0:T(8,128)(2,1)S(1)}, bf16[128,2048]{1,0:T(8,128)(2,1)S(1)}, s32[]{:T(128)}, ...), condition=%wide.region_6.7_spmd, body=%wide.region_5.6_spmd.sunk | while | flops 134742016 | bytes 14765141 | solution.py:100
  234.6 4.0 rev.9
  239.2 5.0 %dynamic_update_slice.10 = f32[8,257,128]{2,0,1:T(8,128)} dynamic-update-slice(f32[8,257,128]{2,0,1:T(8,128)} %get-tuple-element.142, f32[1,257,128]{2,0,1:T(1,128)S(1)} %copy.62, s32[]{:T(128)} %get-tuple-element.141, s32[]{:T(128)} %constant.54.clone.1..sunk.1, s32[]{:T(128)} %constant.54.clone.1..sunk.1) | dynamic-update-slice | bytes 263172 | tf_op jit(solution)/shard_map/while/body/jit(dynamic_update_index_in_dim)/dynamic_update_slice | solution.py:100
  248.1 4.0 rev.9
  252.7 5.0 %dynamic_update_slice.10 = f32[8,257,128]{2,0,1:T(8,128)} dynamic-update-slice(f32[8,257,128]{2,0,1:T(8,128)} %get-tuple-element.142, f32[1,257,128]{2,0,1:T(1,128)S(1)} %copy.62, s32[]{:T(128)} %get-tuple-element.141, s32[]{:T(128)} %constant.54.clone.1..sunk.1, s32[]{:T(128)} %constant.54.clone.1..sunk.1) | dynamic-update-slice | bytes 263172 | tf_op jit(solution)/shard_map/while/body/jit(dynamic_update_index_in_dim)/dynamic_update_slice | solution.py:100
  266.2 5.0 %dynamic_update_slice.10 = f32[8,257,128]{2,0,1:T(8,128)} dynamic-update-slice(f32[8,257,128]{2,0,1:T(8,128)} %get-tuple-element.142, f32[1,257,128]{2,0,1:T(1,128)S(1)} %copy.62, s32[]{:T(128)} %get-tuple-element.141, s32[]{:T(128)} %constant.54.clone.1..sunk.1, s32[]{:T(128)} %constant.54.clone.1..sunk.1) | dynamic-update-slice | bytes 263172 | tf_op jit(solution)/shard_map/while/body/jit(dynamic_update_index_in_dim)/dynamic_update_slice | solution.py:100
  279.7 5.0 %dynamic_update_slice.10 = f32[8,257,128]{2,0,1:T(8,128)} dynamic-update-slice(f32[8,257,128]{2,0,1:T(8,128)} %get-tuple-element.142, f32[1,257,128]{2,0,1:T(1,128)S(1)} %copy.62, s32[]{:T(128)} %get-tuple-element.141, s32[]{:T(128)} %constant.54.clone.1..sunk.1, s32[]{:T(128)} %constant.54.clone.1..sunk.1) | dynamic-update-slice | bytes 263172 | tf_op jit(solution)/shard_map/while/body/jit(dynamic_update_index_in_dim)/dynamic_update_slice | solution.py:100
  293.3 5.0 %dynamic_update_slice.10 = f32[8,257,128]{2,0,1:T(8,128)} dynamic-update-slice(f32[8,257,128]{2,0,1:T(8,128)} %get-tuple-element.142, f32[1,257,128]{2,0,1:T(1,128)S(1)} %copy.62, s32[]{:T(128)} %get-tuple-element.141, s32[]{:T(128)} %constant.54.clone.1..sunk.1, s32[]{:T(128)} %constant.54.clone.1..sunk.1) | dynamic-update-slice | bytes 263172 | tf_op jit(solution)/shard_map/while/body/jit(dynamic_update_index_in_dim)/dynamic_update_slice | solution.py:100
  306.8 5.0 %dynamic_update_slice.10 = f32[8,257,128]{2,0,1:T(8,128)} dynamic-update-slice(f32[8,257,128]{2,0,1:T(8,128)} %get-tuple-element.142, f32[1,257,128]{2,0,1:T(1,128)S(1)} %copy.62, s32[]{:T(128)} %get-tuple-element.141, s32[]{:T(128)} %constant.54.clone.1..sunk.1, s32[]{:T(128)} %constant.54.clone.1..sunk.1) | dynamic-update-slice | bytes 263172 | tf_op jit(solution)/shard_map/while/body/jit(dynamic_update_index_in_dim)/dynamic_update_slice | solution.py:100
  320.3 5.0 %dynamic_update_slice.10 = f32[8,257,128]{2,0,1:T(8,128)} dynamic-update-slice(f32[8,257,128]{2,0,1:T(8,128)} %get-tuple-element.142, f32[1,257,128]{2,0,1:T(1,128)S(1)} %copy.62, s32[]{:T(128)} %get-tuple-element.141, s32[]{:T(128)} %constant.54.clone.1..sunk.1, s32[]{:T(128)} %constant.54.clone.1..sunk.1) | dynamic-update-slice | bytes 263172 | tf_op jit(solution)/shard_map/while/body/jit(dynamic_update_index_in_dim)/dynamic_update_slice | solution.py:100
  333.8 5.0 %dynamic_update_slice.10 = f32[8,257,128]{2,0,1:T(8,128)} dynamic-update-slice(f32[8,257,128]{2,0,1:T(8,128)} %get-tuple-element.142, f32[1,257,128]{2,0,1:T(1,128)S(1)} %copy.62, s32[]{:T(128)} %get-tuple-element.141, s32[]{:T(128)} %constant.54.clone.1..sunk.1, s32[]{:T(128)} %constant.54.clone.1..sunk.1) | dynamic-update-slice | bytes 263172 | tf_op jit(solution)/shard_map/while/body/jit(dynamic_update_index_in_dim)/dynamic_update_slice | solution.py:100
  343.9 61.5 %all-reduce.5.cloned.1.call-done = f32[2,8,257,128]{3,1,2,0:T(8,128)} async-done(((f32[2,8,257,128]{3,1,2,0:T(8,128)}), f32[2,8,257,128]{3,1,2,0:T(8,128)}) %all-reduce.5.cloned.1.call-update) | async-done | bytes 2105360
  (197 shorter events, 139.7 us)
Async XLA Ops:
  6.5 8.2 %copy-start.1 = (bf16[64]{0:T(256)(128)(2,1)S(1)}, bf16[64]{0:T(256)(128)(2,1)}, u32[]{:S(2)}) copy-start(bf16[64]{0:T(256)(128)(2,1)} %param.8) | copy-start | bytes 388
  6.5 8.3 %copy-start = (s32[2,8]{1,0:T(2,128)S(1)}, s32[2,8]{1,0:T(2,128)}, u32[]{:S(2)}) copy-start(s32[2,8]{1,0:T(2,128)} %param.9) | copy-start | bytes 196
  6.5 69.1 %all-gather.5.cloned.1.call-start = ((), (), s32[]{:S(2)}) async-start(), calls=%async_computation | async-start | bytes 1114112 | tf_op jit(solution)/shard_map/all_gather | solution.py:121
  9.8 12.0 %collective-permute-start = (bf16[128,64]{0,1:T(8,128)(2,1)S(1)}, bf16[128,64]{0,1:T(8,128)(2,1)S(1)}, u32[]{:S(2)}, u32[]{:S(2)}) collective-permute-start(bf16[128,64]{0,1:T(8,128)(2,1)S(1)} %slice.86), channel_id=1, source_target_pairs={{0,1},{2,3},{4,5},{6,7},{8,9},{10,11},{12,13},{14,15},{16,17},{18,... | collective-permute-start | bytes 49160 | tf_op jit(solution)/shard_map/ppermute | solution.py:19
  25.6 3.0 collective-permute-start.1
  26.9 5.6 %collective-permute-start.2 = (f32[128,32]{0,1:T(8,128)S(1)}, f32[128,32]{0,1:T(8,128)S(1)}, u32[]{:S(2)}, u32[]{:S(2)}) collective-permute-start(f32[128,32]{0,1:T(8,128)S(1)} %get-tuple-element.72), channel_id=1, source_target_pairs={{1,0},{3,2},{5,4},{7,6},{9,8},{11,10},{13,12},{15,14},{17,16},{19,... | collective-permute-start | bytes 49160 | tf_op jit(solution)/shard_map/ppermute | solution.py:30
  37.3 77.4 %all-gather.7.cloned.1.call-start = ((), (), s32[]{:S(2)}) async-start(), calls=%async_computation.1 | async-start | bytes 1114112 | tf_op jit(solution)/shard_map/all_gather | solution.py:121
  38.2 367.1 %all-reduce.5.cloned.1.call-start = ((), (), s32[]{:S(2)}) async-start(), calls=%async_computation.2 | async-start | bytes 4210688
  77.0 43.9 %collective-permute-start.3 = (bf16[8,128]{1,0:T(8,128)(2,1)S(1)}, bf16[8,128]{1,0:T(8,128)(2,1)S(1)}, u32[]{:S(2)}, u32[]{:S(2)}) collective-permute-start(bf16[8,128]{1,0:T(8,128)(2,1)S(1)} %get-tuple-element.73), channel_id=1, source_target_pairs={{0,1},{2,3},{4,5},{6,7},{8,9},{10,11},{12,13},{14,15},{16,17},{18,... | collective-permute-start | bytes 6152 | tf_op jit(solution)/shard_map/ppermute | solution.py:29
  80.3 40.5 %collective-permute-start.4 = (bf16[8,128]{1,0:T(8,128)(2,1)S(1)}, bf16[8,128]{1,0:T(8,128)(2,1)S(1)}, u32[]{:S(2)}, u32[]{:S(2)}) collective-permute-start(bf16[8,128]{1,0:T(8,128)(2,1)S(1)} %get-tuple-element.74), channel_id=1, source_target_pairs={{1,0},{3,2},{5,4},{7,6},{9,8},{11,10},{13,12},{15,14},{17,16},{19,... | collective-permute-start | bytes 6152 | tf_op jit(solution)/shard_map/ppermute | solution.py:30
  116.0 113.7 %collective-permute-start.5 = (bf16[8,128]{1,0:T(8,128)(2,1)S(1)}, bf16[8,128]{1,0:T(8,128)(2,1)S(1)}, u32[]{:S(2)}, u32[]{:S(2)}) collective-permute-start(bf16[8,128]{1,0:T(8,128)(2,1)S(1)} %get-tuple-element.75), channel_id=1, source_target_pairs={{0,1},{2,3},{4,5},{6,7},{8,9},{10,11},{12,13},{14,15},{16,17},{18,... | collective-permute-start | bytes 6152 | tf_op jit(solution)/shard_map/ppermute | solution.py:29
  119.4 110.3 %collective-permute-start.6 = (bf16[8,128]{1,0:T(8,128)(2,1)S(1)}, bf16[8,128]{1,0:T(8,128)(2,1)S(1)}, u32[]{:S(2)}, u32[]{:S(2)}) collective-permute-start(bf16[8,128]{1,0:T(8,128)(2,1)S(1)} %get-tuple-element.76), channel_id=1, source_target_pairs={{1,0},{3,2},{5,4},{7,6},{9,8},{11,10},{13,12},{15,14},{17,16},{19,... | collective-permute-start | bytes 6152 | tf_op jit(solution)/shard_map/ppermute | solution.py:30
  342.0 0.7 copy-start.2
Sparse Core Ops, SparseCore 0:
  37.4 38.2 all-gather.4
  77.8 36.8 all-gather.6
  342.1 63.1 all-reduce.4
